TPU v7x, 32 devices: a whole 2x2x4 slice. The times are simulated.
32 devices in a mesh: section: 2 (over core), group: 16 (over z, y, x).
Axes of the slice: x: 2, y: 2, z: 4, core: 2. Of those that a mesh axis runs over, the one named last changes fastest.
Arguments:
- upstream: bfloat16 [2, 256, 8192], P('section', None, 'group'), may hold values from -6 to 6
- projected: bfloat16 [2, 3, 256, 3, 4096], P('section', None, None, None, 'group'), may hold values from -6 to 6
- w_in: bfloat16 [2, 8192, 3, 4096], P('section', None, None, 'group'), may hold values from -0.0546875 to 0.0546875
- w_out: bfloat16 [2, 4096, 8192], P('section', 'group'), may hold values from -0.0625 to 0.0625
- short_filter: float32 [2, 3, 7, 4096], P('section', None, None, 'group'), may hold values from -2 to 2
- long_filter: float32 [2, 128, 4096], P('section', None, 'group'), may hold values from -0.5 to 0.5
Outputs:
- input_grad: bfloat16 [2, 256, 8192], P('section', None, 'group')
- proj_grad: bfloat16 [2, 3, 256, 3, 4096], P('section', None, None, None, 'group')
- long_filter_grad: float32 [2, 128, 4096], P('section', None, 'group')
- short_filter_grad: float32 [2, 3, 7, 4096], P('section', None, None, 'group')
All inputs are finite; a program needn't handle non-finite values.
Results may differ from a plain program's by a relative error of at most 0.033.
Values may be sent and summed in bfloat16 or wider, within the bound.
A program may use at most 128 MiB of HBM per device.

v0:
```python
import jax
import jax.numpy as jnp
from jax import lax
from jax.sharding import PartitionSpec as P

HIGHEST = lax.Precision.HIGHEST


def passed_along(value, axis, steps):
    count = lax.axis_size(axis)
    pairs = [(source, (source + steps) % count) for source in range(count)]
    return lax.ppermute(value, axis, pairs)


def depthwise(operand, kernel):
    result = lax.conv_general_dilated(
        operand[None],
        kernel[:, None, :],
        (1,),
        "VALID",
        dimension_numbers=("NWC", "WIO", "NWC"),
        feature_group_count=operand.shape[1],
        precision=HIGHEST,
    )
    return result[0]


def causal(signal, filter_taps):
    extent = filter_taps.shape[0]
    padded = jnp.pad(signal, ((extent - 1, 0), (0, 0)))
    return depthwise(padded, filter_taps[::-1])


def anticausal(gradient, filter_taps):
    extent = filter_taps.shape[0]
    padded = jnp.pad(gradient, ((0, extent - 1), (0, 0)))
    return depthwise(padded, filter_taps)


def tap_grad(gradient, signal, extent):
    padded = jnp.pad(signal, ((extent - 1, 0), (0, 0)))
    return depthwise(padded, gradient)[::-1]


def mixer_backward(out_grad, projected_rows, short_taps, long_taps):
    signal = projected_rows.astype(jnp.float32)
    query_conv = causal(signal[:, 0], short_taps[0])
    key_conv = causal(signal[:, 1], short_taps[1])
    value_conv = causal(signal[:, 2], short_taps[2])
    gating = key_conv * value_conv
    long_mixed = causal(gating, long_taps)
    mixed_grad = out_grad * query_conv
    query_grad = out_grad * long_mixed
    gating_grad = anticausal(mixed_grad, long_taps)
    key_grad = gating_grad * value_conv
    value_grad = gating_grad * key_conv
    proj_grad = jnp.stack(
        [
            anticausal(query_grad, short_taps[0]),
            anticausal(key_grad, short_taps[1]),
            anticausal(value_grad, short_taps[2]),
        ],
        axis=1,
    ).astype(jnp.bfloat16)
    long_grad = tap_grad(mixed_grad, gating, long_taps.shape[0])
    short_extent = short_taps.shape[1]
    short_grad = jnp.stack(
        [
            tap_grad(query_grad, signal[:, 0], short_extent),
            tap_grad(key_grad, signal[:, 1], short_extent),
            tap_grad(value_grad, signal[:, 2], short_extent),
        ],
        axis=0,
    )
    return (proj_grad, long_grad, short_grad)


def local(upstream, projected, w_in, w_out, short_filter, long_filter):
    rounds = projected.shape[1]
    tokens = projected.shape[2]
    local_ch = projected.shape[4]
    model_width = w_in.shape[1]
    in_flat = w_in[0].reshape(model_width, 3 * local_ch)
    out_rows = w_out[0]
    short_taps = short_filter[0]
    long_taps = long_filter[0]
    contract = (((1,), (1,)), ((), ()))
    incoming = upstream[0]
    grad_list = []
    long_total = jnp.zeros(long_taps.shape, jnp.float32)
    short_total = jnp.zeros(short_taps.shape, jnp.float32)
    for round_index in range(rounds):
        final_round = round_index == rounds - 1
        if round_index == 0:
            out_grad = lax.dot_general(
                lax.all_gather(incoming, "group", axis=1, tiled=True),
                out_rows,
                contract,
                preferred_element_type=jnp.float32,
            )
        else:
            out_grad = lax.dot_general(
                lax.all_gather(incoming, "group", axis=0, tiled=True),
                out_rows,
                contract,
                preferred_element_type=jnp.float32,
            )
        proj_grad, long_grad, short_grad = mixer_backward(
            out_grad, projected[0, round_index], short_taps, long_taps
        )
        grad_list.append(proj_grad)
        long_total = long_total + long_grad
        short_total = short_total + short_grad
        grad_flat = proj_grad.reshape(tokens, 3 * local_ch)
        if final_round:
            partial_sums = lax.dot_general(
                grad_flat, in_flat, contract, preferred_element_type=jnp.float32
            )
            outgoing = lax.psum_scatter(
                partial_sums.astype(jnp.bfloat16), "group", scatter_dimension=1, tiled=True
            ).astype(jnp.float32)
        else:
            outgoing = lax.psum_scatter(
                lax.dot_general(
                    grad_flat, in_flat, contract, preferred_element_type=jnp.float32
                ).astype(jnp.bfloat16),
                "group",
                scatter_dimension=0,
                tiled=True,
            ).astype(jnp.float32)
        incoming = passed_along(outgoing.astype(jnp.bfloat16), "section", -1)
    return (incoming[None], jnp.stack(grad_list)[None], long_total[None], short_total[None])


def solution(mesh):
    in_specs = (
        P("section", None, "group"),
        P("section", None, None, None, "group"),
        P("section", None, None, "group"),
        P("section", "group", None),
        P("section", None, None, "group"),
        P("section", None, "group"),
    )
    out_specs = (
        P("section", None, "group"),
        P("section", None, None, None, "group"),
        P("section", None, "group"),
        P("section", None, None, "group"),
    )
    return jax.shard_map(local, mesh=mesh, in_specs=in_specs, out_specs=out_specs, check_vma=False)
```

profile of v0, /device:TPU:0, one launch (start us, length us, event | category | flops | bytes accessed | tf_op | source)
XLA Modules:
  0.0 620.2 jit_solution(12517190076704536715)
XLA Ops:
  21.1 16.7 %copy.88 = bf16[1,8192,3,256]{1,3,2,0:T(8,128)(2,1)} copy(bf16[1,8192,3,256]{3,1,2,0:T(8,128)(2,1)} %param.8) | data formatting | bytes 25165824 | tf_op args[2]
  37.8 3.4 fusion.180
  41.3 53.4 %all-gather.9.cloned.1.call-done = bf16[1,256,8192]{2,1,0:T(8,128)(2,1)} async-done(((bf16[1,256,512]{2,1,0:T(8,128)(2,1)}), bf16[1,256,8192]{2,1,0:T(8,128)(2,1)}) %all-gather.9.cloned.1.call-update) | async-done | bytes 4194320 | tf_op jit(solution)/shard_map/all_gather | solution.py:96
  94.6 5.5 bitcast_multiply_fusion.2
  102.1 4.6 slice_multiply_fusion.5
  111.2 9.7 %convolution_convert_fusion.2 = bf16[256,8192]{1,0:T(8,128)(2,1)} fusion(bf16[256,768]{0,1:T(8,128)(2,1)S(1)} %bitcast.355, bf16[8192,768]{0,1:T(8,128)(2,1)} %bitcast.351), kind=kOutput, calls=%fused_computation.2 | convolution fusion | flops 3223322624 | bytes 17170432 | tf_op jit(solution)/shard_map/dot_general | solution.py:124
  121.0 93.4 %reduce-scatter.4.cloned.1.call-done = bf16[16,8192]{1,0:T(8,128)(2,1)} async-done(((bf16[256,8192]{1,0:T(8,128)(2,1)}), bf16[16,8192]{1,0:T(8,128)(2,1)}) %reduce-scatter.4.cloned.1.call-update) | async-done | bytes 262160 | tf_op jit(solution)/shard_map/reduce_scatter | solution.py:123
  225.7 2.8 fusion.178
  228.5 64.3 %all-gather.5.cloned.1.call-done = bf16[256,8192]{1,0:T(8,128)(2,1)} async-done(((bf16[16,8192]{1,0:T(8,128)(2,1)}), bf16[256,8192]{1,0:T(8,128)(2,1)}) %all-gather.5.cloned.1.call-update) | async-done | bytes 4194320 | tf_op jit(solution)/shard_map/all_gather | solution.py:103
  292.9 5.5 bitcast_multiply_fusion.1
  299.7 4.6 slice_multiply_fusion.3
  308.1 9.7 %convolution_convert_fusion.1 = bf16[256,8192]{1,0:T(8,128)(2,1)} fusion(bf16[256,768]{0,1:T(8,128)(2,1)S(1)} %bitcast.356, bf16[8192,768]{0,1:T(8,128)(2,1)} %bitcast.352), kind=kOutput, calls=%fused_computation.1 | convolution fusion | flops 3223322624 | bytes 17170432 | tf_op jit(solution)/shard_map/dot_general | solution.py:124
  317.9 93.8 %reduce-scatter.6.cloned.1.call-done = bf16[16,8192]{1,0:T(8,128)(2,1)} async-done(((bf16[256,8192]{1,0:T(8,128)(2,1)}), bf16[16,8192]{1,0:T(8,128)(2,1)}) %reduce-scatter.6.cloned.1.call-update) | async-done | bytes 262160 | tf_op jit(solution)/shard_map/reduce_scatter | solution.py:123
  423.1 3.9 fusion.176
  427.0 63.1 %all-gather.7.cloned.1.call-done = bf16[256,8192]{1,0:T(8,128)(2,1)} async-done(((bf16[16,8192]{1,0:T(8,128)(2,1)}), bf16[256,8192]{1,0:T(8,128)(2,1)}) %all-gather.7.cloned.1.call-update) | async-done | bytes 4194320 | tf_op jit(solution)/shard_map/all_gather | solution.py:103
  490.1 5.5 bitcast_multiply_fusion
  498.5 4.6 slice_multiply_fusion.1
  507.0 9.7 %convolution_convert_fusion = bf16[256,8192]{1,0:T(8,128)(2,1)} fusion(bf16[256,768]{0,1:T(8,128)(2,1)S(1)} %bitcast.354, bf16[8192,768]{0,1:T(8,128)(2,1)} %bitcast.353), kind=kOutput, calls=%fused_computation | convolution fusion | flops 3223322624 | bytes 17170432 | tf_op jit(solution)/shard_map/dot_general | solution.py:116
  521.1 8.7 %fusion.119 = f32[1,7,256]{2,0,1:T(1,128)S(1)} fusion(f32[1,262,256]{2,0,1:T(1,128)S(1)} %broadcast_in_dim.145, f32[256,1,256]{2,0,1:T(8,128)S(1)} %bitcast.360), kind=kOutput, calls=%fused_computation.196 | convolution fusion | flops 5505024 | bytes 537600 | tf_op jit(solution)/shard_map/conv_general_dilated | solution.py:16
  532.4 3.3 fusion.123
  535.9 8.8 %fusion.117 = f32[1,7,256]{2,0,1:T(1,128)S(1)} fusion(f32[1,262,256]{2,0,1:T(1,128)S(1)} %broadcast_in_dim.154, f32[256,1,256]{2,0,1:T(8,128)S(1)} %bitcast.362), kind=kOutput, calls=%fused_computation.194 | convolution fusion | flops 5505024 | bytes 537600 | tf_op jit(solution)/shard_map/conv_general_dilated | solution.py:16
  546.7 2.6 fusion.121
  549.5 8.8 %fusion.115 = f32[1,7,256]{2,0,1:T(1,128)S(1)} fusion(f32[1,262,256]{2,0,1:T(1,128)S(1)} %copy-done.1, f32[256,1,256]{2,0,1:T(8,128)S(1)} %bitcast.364), kind=kOutput, calls=%fused_computation.192 | convolution fusion | flops 5505024 | bytes 537600 | tf_op jit(solution)/shard_map/conv_general_dilated | solution.py:16
  560.7 49.9 %reduce-scatter.8.cloned.1.call-done = bf16[256,512]{1,0:T(8,128)(2,1)} async-done(((bf16[256,8192]{1,0:T(8,128)(2,1)}), bf16[256,512]{1,0:T(8,128)(2,1)}) %reduce-scatter.8.cloned.1.call-update) | async-done | bytes 262160 | tf_op jit(solution)/shard_map/reduce_scatter | solution.py:119
  (342 shorter events, 67.9 us)
Async XLA Ops:
  7.2 87.5 %all-gather.9.cloned.1.call-start = ((), (), s32[]{:S(2)}) async-start(), calls=%async_computation.8 | async-start | bytes 4456448 | tf_op jit(solution)/shard_map/all_gather | solution.py:96
  7.9 206.5 %reduce-scatter.4.cloned.1.call-start = ((), (), s32[]{:S(2)}) async-start(), calls=%async_computation.3 | async-start | bytes 4456448 | tf_op jit(solution)/shard_map/reduce_scatter | solution.py:123
  18.9 18.9 %copy-start.25 = (f32[1,383,256]{2,0,1:T(1,128)}, f32[1,383,256]{2,0,1:T(1,128)S(1)}, u32[]{:S(2)}) copy-start(f32[1,383,256]{2,0,1:T(1,128)S(1)} %broadcast_in_dim.142) | copy-start | bytes 1176580
  21.1 16.7 %copy-start.44 = (f32[128,256]{1,0:T(8,128)S(1)}, f32[128,256]{1,0:T(8,128)}, u32[]{:S(2)}) copy-start(f32[128,256]{1,0:T(8,128)} %rev.58) | copy-start | bytes 393220
  41.3 59.9 %copy-start.46 = (f32[1,3,7,256]{3,0,2,1:T(1,128)S(1)}, f32[1,3,7,256]{3,0,2,1:T(1,128)}, u32[]{:S(2)}) copy-start(f32[1,3,7,256]{3,0,2,1:T(1,128)} %param.10) | copy-start | bytes 64516
  120.9 171.9 %all-gather.5.cloned.1.call-start = ((), (), s32[]{:S(2)}) async-start(), calls=%async_computation.4 | async-start | bytes 4456448 | tf_op jit(solution)/shard_map/all_gather | solution.py:103
  214.4 1.7 collective-permute-start
  216.9 194.9 %reduce-scatter.6.cloned.1.call-start = ((), (), s32[]{:S(2)}) async-start(), calls=%async_computation.5 | async-start | bytes 4456448 | tf_op jit(solution)/shard_map/reduce_scatter | solution.py:123
  317.8 97.9 %copy-start.11 = (f32[256,256]{1,0:T(8,128)S(1)}, f32[256,256]{1,0:T(8,128)}, u32[]{:S(2)}) copy-start(f32[256,256]{1,0:T(8,128)} %get-tuple-element.17) | copy-start | bytes 786436
  317.9 172.2 %all-gather.7.cloned.1.call-start = ((), (), s32[]{:S(2)}) async-start(), calls=%async_computation.6 | async-start | bytes 4456448 | tf_op jit(solution)/shard_map/all_gather | solution.py:103
  411.8 1.7 collective-permute-start.1
  414.2 196.4 %reduce-scatter.8.cloned.1.call-start = ((), (), s32[]{:S(2)}) async-start(), calls=%async_computation.7 | async-start | bytes 4456448 | tf_op jit(solution)/shard_map/reduce_scatter | solution.py:119
  423.1 67.0 %copy-start.2 = (f32[1,264,256]{2,1,0:T(8,128)S(1)}, f32[1,264,256]{2,1,0:T(8,128)}, u32[]{:S(2)}) copy-start(f32[1,264,256]{2,1,0:T(8,128)} %reshape.548) | copy-start | bytes 811012
  520.4 12.0 %copy-start.10 = (f32[256,256]{1,0:T(8,128)S(1)}, f32[256,256]{1,0:T(8,128)}, u32[]{:S(2)}) copy-start(f32[256,256]{1,0:T(8,128)} %get-tuple-element.29) | copy-start | bytes 786436
  532.4 12.6 %copy-start.38 = (f32[1,256,256]{2,0,1:T(1,128)S(1)}, f32[1,256,256]{2,0,1:T(1,128)}, u32[]{:S(2)}) copy-start(f32[1,256,256]{2,0,1:T(1,128)} %copy-done.37) | copy-start | bytes 786436
  549.3 62.0 %copy-start.16 = (bf16[1,256,1,256]{3,1,2,0:T(8,128)(2,1)S(1)}, bf16[1,256,1,256]{3,1,2,0:T(8,128)(2,1)}, u32[]{:S(2)}) copy-start(bf16[1,256,1,256]{3,1,2,0:T(8,128)(2,1)} %get-tuple-element.36) | copy-start | bytes 393220
  549.3 61.9 %copy-start.17 = (bf16[1,256,1,256]{3,1,2,0:T(8,128)(2,1)S(1)}, bf16[1,256,1,256]{3,1,2,0:T(8,128)(2,1)}, u32[]{:S(2)}) copy-start(bf16[1,256,1,256]{3,1,2,0:T(8,128)(2,1)} %get-tuple-element.38) | copy-start | bytes 393220
  549.3 61.9 %copy-start.18 = (bf16[1,256,1,256]{3,1,2,0:T(8,128)(2,1)S(1)}, bf16[1,256,1,256]{3,1,2,0:T(8,128)(2,1)}, u32[]{:S(2)}) copy-start(bf16[1,256,1,256]{3,1,2,0:T(8,128)(2,1)} %get-tuple-element.40) | copy-start | bytes 393220
  549.3 61.9 %copy-start.19 = (bf16[1,256,1,256]{3,1,2,0:T(8,128)(2,1)S(1)}, bf16[1,256,1,256]{3,1,2,0:T(8,128)(2,1)}, u32[]{:S(2)}) copy-start(bf16[1,256,1,256]{3,1,2,0:T(8,128)(2,1)} %get-tuple-element.42) | copy-start | bytes 393220
  549.3 61.9 %copy-start.20 = (bf16[1,256,1,256]{3,1,2,0:T(8,128)(2,1)S(1)}, bf16[1,256,1,256]{3,1,2,0:T(8,128)(2,1)}, u32[]{:S(2)}) copy-start(bf16[1,256,1,256]{3,1,2,0:T(8,128)(2,1)} %get-tuple-element.44) | copy-start | bytes 393220
  549.3 61.9 %copy-start.21 = (bf16[1,256,1,256]{3,1,2,0:T(8,128)(2,1)S(1)}, bf16[1,256,1,256]{3,1,2,0:T(8,128)(2,1)}, u32[]{:S(2)}) copy-start(bf16[1,256,1,256]{3,1,2,0:T(8,128)(2,1)} %get-tuple-element.48) | copy-start | bytes 393220
  549.4 61.9 %copy-start.22 = (bf16[1,256,1,256]{3,1,2,0:T(8,128)(2,1)S(1)}, bf16[1,256,1,256]{3,1,2,0:T(8,128)(2,1)}, u32[]{:S(2)}) copy-start(bf16[1,256,1,256]{3,1,2,0:T(8,128)(2,1)} %get-tuple-element.50) | copy-start | bytes 393220
  549.4 61.9 %copy-start.23 = (bf16[1,256,1,256]{3,1,2,0:T(8,128)(2,1)S(1)}, bf16[1,256,1,256]{3,1,2,0:T(8,128)(2,1)}, u32[]{:S(2)}) copy-start(bf16[1,256,1,256]{3,1,2,0:T(8,128)(2,1)} %get-tuple-element.52) | copy-start | bytes 393220
  610.6 1.9 collective-permute-start.2
  (33 other events, 128.2 us)
Sparse Core Ops, SparseCore 0:
  10.7 83.8 all-gather.8
  121.0 93.3 reduce-scatter.3
  217.2 75.6 all-gather.4
  318.0 93.7 reduce-scatter.5
  414.4 75.6 all-gather.6
  516.8 93.7 reduce-scatter.7
where the time goes:
time: 630 us; the launch traced here: 620 us
  waiting for transfers between devices  422 us (67%)
  matrix products  116 us (18%)
  local copies, waits for them, and re-layouts  61.8 us (10%)
  between operations  16.1 us (3%)
    reduce_scatter x2, waiting for transfers between devices, local(): lax.psum_scatter(lax.dot_general(grad_flat, in_flat, contract, preferred_...  187 us
    all_gather x2, waiting for transfers between devices, local(): lax.all_gather(incoming, 'group', axis=0, tiled=True)  127 us
    conv_general_dilated x36, matrix products, depthwise(): lax.conv_general_dilated(operand[None], kernel[:, None, :], (1,), 'VALID'...  70.5 us
    all_gather x1, waiting for transfers between devices, local(): lax.all_gather(incoming, 'group', axis=1, tiled=True)  53.4 us
    reduce_scatter x1, waiting for transfers between devices, local(): lax.psum_scatter(partial_sums.astype(jnp.bfloat16), 'group', scatter_dime...  49.9 us
    dot_general x3, matrix products, local(): lax.dot_general(grad_flat, in_flat, contract, preferred_element_type=jnp....  29.2 us
    unnamed x119, local copies, waits for them, and re-layouts  27.6 us
    conv_general_dilated x69, local copies, waits for them, and re-layouts, depthwise(): lax.conv_general_dilated(operand[None], kernel[:, None, :], (1,), 'VALID'...  15.5 us
  transfers between devices with their start and end apart: 9, of which 8 were waited for; matrix products, arithmetic and copies ran while one was open for 16% of the time, Pallas kernels for 0%

commit v1 on v0

v1 whole, which is shorter than its diff:
```python
import functools

import jax
import jax.numpy as jnp
from jax import lax
from jax.experimental import pallas as pl
from jax.experimental.pallas import tpu as pltpu
from jax.sharding import PartitionSpec as P

NT = (((1,), (1,)), ((), ()))


LANES = 128
PAD = 8


def mixers_body(
    line,
    sections,
    first_ref,
    projected_ref,
    w_in_any,
    w_out_any,
    short_ref,
    long_ref,
    result_ref,
    proj_ref,
    long_out,
    short_out,
    w_in_ref,
    w_out_ref,
    weight_sems,
    part,
    got_p,
    got_q,
    got_up,
    got_down,
    sum_ref,
    turned,
    landed,
    total,
    signal,
    conv,
    gating,
    mixed,
    mixed_grad,
    grads,
    long_part,
    short_part,
    p_send,
    p_recv,
    q_send,
    q_recv,
    up_send,
    up_recv,
    down_send,
    down_recv,
    turn_send,
    turn_recv,
    gl_up,
    gl_down,
    gl_recv,
    gq_send,
    gq_recv,
    gp_send,
    gp_recv,
):
    rounds = projected_ref.shape[0]
    tokens = landed.shape[1]
    tiles = conv.shape[1]
    extent = long_ref.shape[0]
    short_extent = short_ref.shape[1]
    chunk = extent // line
    strip = min(tokens, 128)
    w_out_copy = pltpu.make_async_copy(w_out_any, w_out_ref, weight_sems.at[0])
    w_in_copy = pltpu.make_async_copy(w_in_any, w_in_ref, weight_sems.at[1])
    w_out_copy.start()
    w_in_copy.start()
    section = lax.axis_index("section")
    me = lax.axis_index("group")
    a = me // 4
    y = (me // 2) % 2
    x = me % 2
    half_rows = landed.shape[1] // 2

    def block(t, yy, xx):
        return t * 4 + yy * 2 + xx

    to_x = {"group": block(a, y, 1 - x)}
    to_y = {"group": block(a, 1 - y, x)}
    above = {"group": lax.rem(me + 4, 4 * line)}
    below = {"group": lax.rem(me + 4 * line - 4, 4 * line)}
    to_section = {"section": lax.rem(section + sections - 1, sections)}
    from_section = {"section": lax.rem(section + 1, sections)}
    not_top = a < line - 1
    not_bottom = a > 0

    barrier = pltpu.get_barrier_semaphore()

    def greet(device):
        pl.semaphore_signal(barrier, inc=1, device_id=device, device_id_type=pl.DeviceIdType.MESH)

    greet(to_x)
    greet(to_y)
    pl.when(not_top)(lambda: greet(above))
    pl.when(not_bottom)(lambda: greet(below))
    greet(from_section)
    ends = 2 + jnp.where(not_top, 1, 0) + jnp.where(not_bottom, 1, 0)
    pl.semaphore_wait(barrier, ends + 1)

    def far_first(k):
        low = line - 1 - k
        low = jnp.where(low <= a, low - 1, low)
        high = jnp.where(k >= a, k + 1, k)
        other = jnp.where(a < line // 2, low, high)
        return jnp.where(k == line - 1, a, other)

    def near_first(k):
        return far_first(line - 1 - k)

    def rows(half):
        return pl.ds(half * half_rows, half_rows)

    def copy(source, target, send, recv, device):
        return pltpu.make_async_remote_copy(
            src_ref=source,
            dst_ref=target,
            send_sem=send,
            recv_sem=recv,
            device_id=device,
            device_id_type=pl.DeviceIdType.MESH,
        )

    def sides(half):
        if half == 0:
            return y, x, to_y, to_x, lambda t, pp, qq: block(t, pp, qq)
        return x, y, to_x, to_y, lambda t, pp, qq: block(t, qq, pp)

    width = part.shape[2]

    def p_copy(half, t, qq):
        p, q, p_dev, q_dev, at = sides(half)
        slot = t * 2 + qq
        return copy(
            part.at[at(t, 1 - p, qq), rows(half)],
            got_p.at[half, slot],
            p_send.at[half, slot],
            p_recv.at[half, slot],
            p_dev,
        )

    def q_copy(half, t):
        p, q, p_dev, q_dev, at = sides(half)
        return copy(
            part.at[at(t, p, 1 - q), rows(half)],
            got_q.at[half, t],
            q_send.at[half, t],
            q_recv.at[half, t],
            q_dev,
        )

    def up_copy(half, t):
        return copy(
            part.at[block(t, y, x), rows(half)], got_up.at[half, t], up_send.at[half, t], up_recv.at[half, t], above
        )

    def down_copy(half, t):
        return copy(
            part.at[block(t, y, x), rows(half)],
            got_down.at[half, t],
            down_send.at[half, t],
            down_recv.at[half, t],
            below,
        )

    def turn_copy(half, r):
        return copy(
            part.at[me, rows(half)], turned.at[r, rows(half)], turn_send.at[half, r], turn_recv.at[half, r], to_section
        )

    depth = landed.shape[2]

    def gl_copy(half, t, send, device):
        piece = landed.at[block(t, y, x), rows(half)]
        return copy(piece, piece, send.at[half, t], gl_recv.at[half, t], device)

    def gq_copy(half, t, arriving):
        p, q, p_dev, q_dev, at = sides(half)
        piece = landed.at[at(t, p, 1 - q if arriving else q), rows(half)]
        return copy(piece, piece, gq_send.at[half, t], gq_recv.at[half, t], q_dev)

    def gp_copy(half, t, qq, arriving):
        p, q, p_dev, q_dev, at = sides(half)
        piece = landed.at[at(t, 1 - p if arriving else p, qq), rows(half)]
        slot = t * 2 + qq
        return copy(piece, piece, gp_send.at[half, slot], gp_recv.at[half, slot], p_dev)

    def add_block(b):
        columns = pl.ds(pl.multiple_of(b * depth, depth), depth)
        total[...] += lax.dot_general(landed[b], w_out_ref[:, columns], NT, preferred_element_type=jnp.float32)


    def lanes(ct):
        return slice(ct * LANES, (ct + 1) * LANES)

    def short_convs(r):
        for ct in range(tiles):
            for i in range(3):
                signal[i, ct, PAD:] = projected_ref[r, i, :, lanes(ct)].astype(jnp.float32)
                value = short_ref[i, 0:1, lanes(ct)] * signal[i, ct, PAD:]
                for j in range(1, short_extent):
                    value += short_ref[i, j : j + 1, lanes(ct)] * signal[i, ct, PAD - j : PAD - j + tokens]
                conv[i, ct] = value
            gating[ct, extent:] = conv[1, ct] * conv[2, ct]
            mixed[ct] = jnp.zeros((tokens, LANES), jnp.float32)

    def tap_sum(source, ct, base, step, first, count, start):
        def eight(n, running):
            base_tap = pl.multiple_of(first + n * 8, 8)
            weights = long_ref[pl.ds(base_tap, 8), lanes(ct)]
            for jj in range(8):
                j = base_tap + jj
                running += weights[jj : jj + 1] * source[ct, pl.ds(base + step * j, strip)]
            return running

        return lax.fori_loop(0, count // 8, eight, start)

    def long_conv(k):
        for ct in range(tiles):
            for t0 in range(0, tokens, strip):
                mixed[ct, t0 : t0 + strip] = tap_sum(
                    gating, ct, extent + t0, -1, k * chunk, chunk, mixed[ct, t0 : t0 + strip]
                )

    def folded(value):
        return value.reshape(value.shape[0] // 8, 8, LANES).sum(axis=0)

    def long_taps_grad(k):
        for ct in range(tiles):
            for t0 in range(0, tokens, strip):
                fixed = mixed_grad[ct, t0 : t0 + strip]

                def four(n, carry):
                    for jj in range(4):
                        j = k * chunk + n * 4 + jj
                        long_part[ct, j] += folded(fixed * gating[ct, pl.ds(extent + t0 - j, strip)])
                    return carry

                lax.fori_loop(0, chunk // 4, four, 0)

    def short_taps_grad():
        for ct in range(tiles):
            for i in range(3):
                for j in range(short_extent):
                    short_part[i, j, ct] += folded(grads[i, ct, :tokens] * signal[i, ct, PAD - j : PAD - j + tokens])

    def mixer(r):
        for ct in range(tiles):
            out_grad = total[:, lanes(ct)]
            mixed_grad[ct, :tokens] = out_grad * conv[0, ct]
            grads[0, ct, :tokens] = out_grad * mixed[ct]
        for ct in range(tiles):
            for t0 in range(0, tokens, strip):
                span = slice(t0, t0 + strip)
                gating_grad = tap_sum(mixed_grad, ct, t0, 1, 0, extent, jnp.zeros((strip, LANES), jnp.float32))
                grads[1, ct, span] = gating_grad * conv[2, ct, span]
                grads[2, ct, span] = gating_grad * conv[1, ct, span]
        for ct in range(tiles):
            for i in range(3):
                value = short_ref[i, 0:1, lanes(ct)] * grads[i, ct, :tokens]
                for j in range(1, short_extent):
                    value += short_ref[i, j : j + 1, lanes(ct)] * grads[i, ct, j : j + tokens]
                proj_ref[r, i, :, lanes(ct)] = value.astype(proj_ref.dtype)

    signal[...] = jnp.zeros_like(signal)
    gating[...] = jnp.zeros_like(gating)
    mixed_grad[...] = jnp.zeros_like(mixed_grad)
    grads[...] = jnp.zeros_like(grads)
    long_part[...] = jnp.zeros_like(long_part)
    short_part[...] = jnp.zeros_like(short_part)
    turned[rounds] = first_ref[...]

    def settle_sum(r):
        def settle(t, carry):
            for half in range(2):
                for qq in range(2):
                    p_copy(half, t, qq).wait_send()
                q_copy(half, t).wait_send()
                pl.when(t > a)(lambda: up_copy(half, t).wait_send())
                pl.when(t < a)(lambda: down_copy(half, t).wait_send())
            return carry

        lax.fori_loop(0, line, settle, 0)
        for half in range(2):
            turn_copy(half, r).wait_send()

    def settle_gather(t, carry):
        for half in range(2):
            pl.when(jnp.logical_and(t <= a, not_top))(lambda: gl_copy(half, t, gl_up, above).wait_send())
            pl.when(jnp.logical_and(t >= a, not_bottom))(lambda: gl_copy(half, t, gl_down, below).wait_send())
            gq_copy(half, t, False).wait_send()
            for qq in range(2):
                gp_copy(half, t, qq, False).wait_send()
        return carry

    def one_round(r, round_carry):
        total[...] = jnp.zeros_like(total)

        def line_step(k, carry):
            t = near_first(k)
            for half in range(2):
                p, q, p_dev, q_dev, at = sides(half)

                @pl.when(t == a)
                def _():
                    pl.when(r > 0)(lambda: turn_copy(half, r - 1).wait_recv())
                    landed[me, rows(half)] = turned[jnp.where(r > 0, r - 1, rounds), rows(half)]

                pl.when(t != a)(lambda: gl_copy(half, t, gl_up, above).wait_recv())
                pl.when(jnp.logical_and(t <= a, not_top))(lambda: gl_copy(half, t, gl_up, above).start())
                pl.when(jnp.logical_and(t >= a, not_bottom))(lambda: gl_copy(half, t, gl_down, below).start())
                gq_copy(half, t, False).start()
                gp_copy(half, t, q, False).start()

            @pl.when(k == 0)
            def _():
                pl.when(r == 0)(lambda: w_out_copy.wait())
                short_convs(r)

            add_block(block(t, y, x))
            return carry

        lax.fori_loop(0, line, line_step, 0)
        pl.when(r > 0)(lambda: settle_sum(r - 1))

        def pass_step(k, carry):
            t = near_first(k)
            for half in range(2):
                p, q, p_dev, q_dev, at = sides(half)
                gq_copy(half, t, True).wait_recv()
                gp_copy(half, t, 1 - q, False).start()
            long_conv(k)
            return carry

        lax.fori_loop(0, line, pass_step, 0)

        def last_step(k, carry):
            t = near_first(k)
            gp_copy(0, t, x, True).wait_recv()
            add_block(block(t, 1 - y, x))
            gp_copy(1, t, y, True).wait_recv()
            add_block(block(t, y, 1 - x))
            gp_copy(0, t, 1 - x, True).wait_recv()
            gp_copy(1, t, 1 - y, True).wait_recv()
            add_block(block(t, 1 - y, 1 - x))
            return carry

        lax.fori_loop(0, line, last_step, 0)
        mixer(r)
        lax.fori_loop(0, line, settle_gather, 0)
        pl.when(r == 0)(lambda: w_in_copy.wait())
        def product(b):
            w_rows = pl.ds(pl.multiple_of(b * width, width), width)
            value = lax.dot_general(proj_ref[r, 0], w_in_ref[0, w_rows, :], NT, preferred_element_type=jnp.float32)
            for i in range(1, 3):
                value += lax.dot_general(proj_ref[r, i], w_in_ref[i, w_rows, :], NT, preferred_element_type=jnp.float32)
            part[b] = value.astype(part.dtype)

        def first_step(k, carry):
            t = far_first(k)
            product(block(t, 1 - y, 1 - x))
            p_copy(0, t, 1 - x).start()
            p_copy(1, t, 1 - y).start()
            product(block(t, 1 - y, x))
            p_copy(0, t, x).start()
            product(block(t, y, 1 - x))
            p_copy(1, t, y).start()
            product(block(t, y, x))
            return carry

        lax.fori_loop(0, line, first_step, 0)

        def second_step(k, carry):
            t = far_first(k)
            for half in range(2):
                p, q, p_dev, q_dev, at = sides(half)
                p_copy(half, t, 1 - q).wait_recv()
                b = at(t, p, 1 - q)
                value = part[b, rows(half)].astype(jnp.float32) + got_p[half, t * 2 + 1 - q].astype(jnp.float32)
                part[b, rows(half)] = value.astype(part.dtype)
                q_copy(half, t).start()
            long_taps_grad(k)
            return carry

        lax.fori_loop(0, line, second_step, 0)
        short_taps_grad()

        def third_step(k, carry):
            t = far_first(k)
            for half in range(2):
                p, q, p_dev, q_dev, at = sides(half)
                p_copy(half, t, q).wait_recv()
                q_copy(half, t).wait_recv()
                b = block(t, y, x)
                total_ref = sum_ref.at[half]
                total_ref[...] = (
                    part[b, rows(half)].astype(jnp.float32)
                    + got_p[half, t * 2 + q].astype(jnp.float32)
                    + got_q[half, t].astype(jnp.float32)
                )

                @pl.when(jnp.logical_and(t >= a, not_bottom))
                def _():
                    up_copy(half, t).wait_recv()
                    total_ref[...] += got_up[half, t].astype(jnp.float32)

                @pl.when(jnp.logical_and(t <= a, not_top))
                def _():
                    down_copy(half, t).wait_recv()
                    total_ref[...] += got_down[half, t].astype(jnp.float32)

                part[b, rows(half)] = total_ref[...].astype(part.dtype)
                pl.when(t > a)(lambda: up_copy(half, t).start())
                pl.when(t < a)(lambda: down_copy(half, t).start())
                pl.when(t == a)(lambda: turn_copy(half, r).start())
            return carry

        lax.fori_loop(0, line, third_step, 0)

        return round_carry

    lax.fori_loop(0, rounds, one_round, 0)
    settle_sum(rounds - 1)
    for ct in range(tiles):
        long_out[:, lanes(ct)] = long_part[ct].sum(axis=1)
        for i in range(3):
            short_out[i, :, lanes(ct)] = short_part[i, :, ct].sum(axis=1)
    for half in range(2):
        turn_copy(half, rounds - 1).wait_recv()
    result_ref[...] = turned[rounds - 1]


def local(upstream, projected, w_in, w_out, short_filter, long_filter):
    rounds = projected.shape[1]
    group = lax.axis_size("group")
    sections = lax.axis_size("section")
    line = group // 4
    _, tokens, width = upstream.shape
    model_width, parts, local_ch = w_in.shape[1:]
    short_extent = short_filter.shape[2]
    extent = long_filter.shape[1]
    tiles = local_ch // LANES
    half_rows = tokens // 2
    dma = pltpu.SemaphoreType.DMA
    vmem16 = lambda *shape: pltpu.VMEM(shape, jnp.bfloat16)
    vmem32 = lambda *shape: pltpu.VMEM(shape, jnp.float32)
    scratch = [
        vmem16(parts, model_width, local_ch),
        vmem16(local_ch, model_width),
        dma((2,)),
        vmem16(group, tokens, width),
        vmem16(2, 2 * line, half_rows, width),
        vmem16(2, line, half_rows, width),
        vmem16(2, line, half_rows, width),
        vmem16(2, line, half_rows, width),
        vmem32(2, half_rows, width),
        vmem16(rounds + 1, tokens, width),
        vmem16(group, tokens, width),
        vmem32(tokens, local_ch),
        vmem32(parts, tiles, PAD + tokens, LANES),
        vmem32(parts, tiles, tokens, LANES),
        vmem32(tiles, extent + tokens, LANES),
        vmem32(tiles, tokens, LANES),
        vmem32(tiles, tokens + extent, LANES),
        vmem32(parts, tiles, tokens + PAD, LANES),
        vmem32(tiles, extent, 8, LANES),
        vmem32(parts, short_extent, tiles, 8, LANES),
    ]
    scratch += [dma((2, 2 * line))] * 2 + [dma((2, line))] * 6 + [dma((2, rounds))] * 2
    scratch += [dma((2, line))] * 5 + [dma((2, 2 * line))] * 2
    vmem = pl.BlockSpec(memory_space=pltpu.VMEM)
    hbm = pl.BlockSpec(memory_space=pl.ANY)
    input_grad, proj_grad, long_grad, short_grad = pl.pallas_call(
        functools.partial(mixers_body, line, sections),
        out_shape=(
            jax.ShapeDtypeStruct((tokens, width), jnp.bfloat16),
            jax.ShapeDtypeStruct((rounds, parts, tokens, local_ch), jnp.bfloat16),
            jax.ShapeDtypeStruct((extent, local_ch), jnp.float32),
            jax.ShapeDtypeStruct((parts, short_extent, local_ch), jnp.float32),
        ),
        in_specs=[vmem, vmem, hbm, hbm, vmem, vmem],
        out_specs=(vmem,) * 4,
        scratch_shapes=scratch,
        compiler_params=pltpu.CompilerParams(
            collective_id=0, has_side_effects=True, vmem_limit_bytes=56 * 2**20
        ),
        name="mixers",
    )(
        upstream[0],
        projected[0].transpose(0, 2, 1, 3),
        w_in[0].transpose(1, 0, 2),
        w_out[0],
        short_filter[0],
        long_filter[0],
    )
    return (input_grad[None], proj_grad.transpose(0, 2, 1, 3)[None], long_grad[None], short_grad[None])


def solution(mesh):
    in_specs = (
        P("section", None, "group"),
        P("section", None, None, None, "group"),
        P("section", None, None, "group"),
        P("section", "group", None),
        P("section", None, None, "group"),
        P("section", None, "group"),
    )
    out_specs = (
        P("section", None, "group"),
        P("section", None, None, None, "group"),
        P("section", None, "group"),
        P("section", None, None, "group"),
    )
    return jax.shard_map(local, mesh=mesh, in_specs=in_specs, out_specs=out_specs, check_vma=False)
```

time: 630 us -> 272 us (0.43); the launches traced: 620 us -> 272 us
  waiting for transfers between devices: 422 us -> 0 us
  Pallas kernels: 0 us -> 264 us
  matrix products: 116 us -> 0 us
  local copies, waits for them, and re-layouts: 61.8 us -> 7.43 us
  between operations: 16.1 us -> 0.64 us
    pallas_call x0 -> x1, Pallas kernels: none -> 264 us  [local(): pl.pallas_call(functools.partial(mixers_body, line, sections), out_shape=...]
    reduce_scatter x3 -> x0, waiting for transfers between devices: 237 us -> none  [the longest x2 187 us: local(): lax.psum_scatter(lax.dot_general(grad_flat, in_flat, contract, preferred_...]
    all_gather x3 -> x0, waiting for transfers between devices: 181 us -> none  [the longest x2 127 us: local(): lax.all_gather(incoming, 'group', axis=0, tiled=True)]
    conv_general_dilated x36 -> x0, matrix products: 70.5 us -> none  [depthwise(): lax.conv_general_dilated(operand[None], kernel[:, None, :], (1,), 'VALID'...]
    dot_general x6 -> x0, matrix products: 45.5 us -> none  [the longest x3 29.2 us: local(): lax.dot_general(grad_flat, in_flat, contract, preferred_element_type=jnp....]
    unnamed x119 -> x7, local copies, waits for them, and re-layouts: 27.6 us -> 7.43 us
    conv_general_dilated x69 -> x0, local copies, waits for them, and re-layouts: 15.5 us -> none  [depthwise(): lax.conv_general_dilated(operand[None], kernel[:, None, :], (1,), 'VALID'...]
    another operation x30 -> x0, local copies, waits for them, and re-layouts: 6.64 us -> none  [the longest x12 5.88 us: mixer_backward(): jnp.stack([anticausal(query_grad, short_taps[0]), anticausal(key_grad, sh...]
  transfers between devices with their start and end apart: 9 -> 0, of which waited for: 8 -> 0; matrix products, arithmetic and copies ran while one was open for 16% -> 0% of each run, Pallas kernels for 0% -> 0%
where the time goes in v1:
time: 272 us
  Pallas kernels  264 us (97%)
  local copies, waits for them, and re-layouts  7.43 us (3%)
    pallas_call x1, Pallas kernels, local(): pl.pallas_call(functools.partial(mixers_body, line, sections), out_shape=...  264 us
    unnamed x7, local copies, waits for them, and re-layouts  7.43 us

profile of v1, /device:TPU:0, one launch (start us, length us, event | category | flops | bytes accessed | tf_op | source)
XLA Modules:
  0.0 272.1 jit_solution(17891933282084785117)
XLA Ops:
  0.6 1.3 copy.13
  2.0 264.0 %mixers.1 = (bf16[256,512]{1,0:T(8,128)(2,1)}, bf16[3,3,256,256]{3,2,1,0:T(8,128)(2,1)}, f32[128,256]{1,0:T(8,128)}, f32[3,7,256]{2,1,0:T(8,128)}) custom-call(bf16[256,512]{1,0:T(8,128)(2,1)} %bitcast.22, bf16[3,3,256,256]{3,2,1,0:T(8,128)(2,1)} %bitcast.20, bf16[3,8192,256]{2,1,0:T(8,128)(2,1)} %bitcast.18, bf16[256,8192]{1,0:T(8,128)(2,1)} %bitcast.19, ...), custom_call_target="tpu_custom_call" | custom-call | tf_op jit(solution)/shard_map/mixers/pallas_call | solution.py:483
  266.0 1.4 copy.10
  267.4 1.7 copy.17
  269.0 0.0 copy-start
  269.0 2.4 copy.18
  271.4 0.0 copy-done
  271.4 0.7 copy.19
Async XLA Ops:
  269.0 2.4 copy-start

commit v2 on v1

--- a/solution.py
+++ b/solution.py
@@ -366,7 +366,7 @@
                 value += lax.dot_general(proj_ref[r, i], w_in_ref[i, w_rows, :], NT, preferred_element_type=jnp.float32)
             part[b] = value.astype(part.dtype)
 
-        def first_step(k, carry):
+        def first_step(k):
             t = far_first(k)
             product(block(t, 1 - y, 1 - x))
             p_copy(0, t, 1 - x).start()
@@ -376,11 +376,9 @@
             product(block(t, y, 1 - x))
             p_copy(1, t, y).start()
             product(block(t, y, x))
-            return carry
-
-        lax.fori_loop(0, line, first_step, 0)
-
-        def second_step(k, carry):
+
+
+        def second_step(k):
             t = far_first(k)
             for half in range(2):
                 p, q, p_dev, q_dev, at = sides(half)
@@ -390,12 +388,10 @@
                 part[b, rows(half)] = value.astype(part.dtype)
                 q_copy(half, t).start()
             long_taps_grad(k)
-            return carry
-
-        lax.fori_loop(0, line, second_step, 0)
-        short_taps_grad()
-
-        def third_step(k, carry):
+            pl.when(k == line - 1)(short_taps_grad)
+
+
+        def third_step(k):
             t = far_first(k)
             for half in range(2):
                 p, q, p_dev, q_dev, at = sides(half)
@@ -423,9 +419,14 @@
                 pl.when(t > a)(lambda: up_copy(half, t).start())
                 pl.when(t < a)(lambda: down_copy(half, t).start())
                 pl.when(t == a)(lambda: turn_copy(half, r).start())
+
+        def staggered(k, carry):
+            pl.when(k < line)(lambda: first_step(k))
+            pl.when(jnp.logical_and(k >= 1, k <= line))(lambda: second_step(k - 1))
+            pl.when(k >= 2)(lambda: third_step(k - 2))
             return carry
 
-        lax.fori_loop(0, line, third_step, 0)
+        lax.fori_loop(0, line + 2, staggered, 0)
 
         return round_carry
 

time: 272 us -> 253 us (0.930)
  Pallas kernels: 264 us -> 245 us
    pallas_call x1, Pallas kernels: 264 us -> 245 us  [local(): pl.pallas_call(functools.partial(mixers_body, line, sections), out_shape=...]
where the time goes in v2:
time: 253 us
  Pallas kernels  245 us (97%)
  local copies, waits for them, and re-layouts  7.43 us (3%)
    pallas_call x1, Pallas kernels, local(): pl.pallas_call(functools.partial(mixers_body, line, sections), out_shape=...  245 us
    unnamed x7, local copies, waits for them, and re-layouts  7.43 us

profile of v2, /device:TPU:0, one launch (start us, length us, event | category | flops | bytes accessed | tf_op | source)
XLA Modules:
  0.0 252.6 jit_solution(1412067707545564980)
XLA Ops:
  0.6 1.3 copy.13
  2.0 244.5 %mixers.1 = (bf16[256,512]{1,0:T(8,128)(2,1)}, bf16[3,3,256,256]{3,2,1,0:T(8,128)(2,1)}, f32[128,256]{1,0:T(8,128)}, f32[3,7,256]{2,1,0:T(8,128)}) custom-call(bf16[256,512]{1,0:T(8,128)(2,1)} %bitcast.22, bf16[3,3,256,256]{3,2,1,0:T(8,128)(2,1)} %bitcast.20, bf16[3,8192,256]{2,1,0:T(8,128)(2,1)} %bitcast.18, bf16[256,8192]{1,0:T(8,128)(2,1)} %bitcast.19, ...), custom_call_target="tpu_custom_call" | custom-call | tf_op jit(solution)/shard_map/mixers/pallas_call | solution.py:484
  246.5 1.4 copy.10
  247.9 1.7 copy.17
  249.5 0.0 copy-start
  249.5 2.4 copy.18
  251.9 0.0 copy-done
  251.9 0.7 copy.19
Async XLA Ops:
  249.5 2.4 copy-start
